TPU v7x, 512 devices: a whole 4x4x16 slice. The times are simulated.
512 devices in a mesh: band: 32 (over x_hi, z), pw: 16 (over y, x_lo, core).
Axes of the slice: x: 4 (x_hi: 2, x_lo: 2; x = x_hi * 2 + x_lo), y: 4, z: 16, core: 2. Of those that a mesh axis runs over, the one named last changes fastest.
Arguments:
- orbitals: float32 [12288, 4096], P('pw', 'band'), may hold values from -0.0546875 to 0.0546875
- h_orbitals: float32 [12288, 4096], P('pw', 'band'), may hold values from -0.0546875 to 0.0546875
Outputs:
- margin_slots: float32 [4096, 2176], P(('band', 'pw'))
- hamilton_slots: float32 [4096, 2176], P(('band', 'pw'))
All inputs are finite; a program needn't handle non-finite values.
Results may differ from a plain program's by a relative error of at most 0.0003.
Values sent between devices are 32-bit elements; how exact they have to be, the bound alone decides.
A program may use at most 64 MiB of HBM per device.

v0:
```python
import jax
import jax.numpy as jnp
from jax import lax
from jax.sharding import PartitionSpec as P


def passed_along(block, axis, distance):
    devices = range(lax.axis_size(axis))
    route = [((i - distance) % len(devices), i) for i in devices]
    return lax.ppermute(block, axis, route)


def shards(orbitals, h_orbitals):
    block_width = orbitals.shape[1]
    band_count = lax.axis_size("band")
    slot_count = band_count // 2 + 1
    stacked = jnp.stack([orbitals, h_orbitals], axis=1)

    def pair_products(shard_piece):
        return jnp.einsum(
            "pb,pmc->mbc",
            orbitals,
            shard_piece,
            precision=lax.Precision.HIGHEST,
            preferred_element_type=jnp.float32,
        )

    def cycle_turn(offset, loop_state):
        current, slot_table = loop_state
        slot_table = lax.dynamic_update_slice_in_dim(
            slot_table, pair_products(current)[:, :, None, :], offset, 2
        )
        current = passed_along(current, "band", -1)
        return (current, slot_table)

    empty_table = jnp.zeros((2, block_width, slot_count, block_width), jnp.float32)
    current, slot_table = lax.fori_loop(0, slot_count - 1, cycle_turn, (stacked, empty_table))
    slot_table = lax.dynamic_update_slice_in_dim(
        slot_table, pair_products(current)[:, :, None, :], slot_count - 1, 2
    )
    partial_value = slot_table.reshape(2, block_width, slot_count * block_width)
    summed = lax.psum_scatter(partial_value, "pw", scatter_dimension=1, tiled=True)
    return (summed[0], summed[1])


def solution(mesh):
    return jax.shard_map(
        shards,
        mesh=mesh,
        in_specs=(P("pw", "band"), P("pw", "band")),
        out_specs=(P(("band", "pw"), None), P(("band", "pw"), None)),
        check_vma=False,
    )
```

profile of v0, /device:TPU:1, one launch (start us, length us, event | category | flops | bytes accessed | tf_op | source)
XLA Modules:
  0.0 507.1 jit_solution(9309985351203342742)
XLA Ops:
  9.7 1.6 broadcast_in_dim.13.clone
  11.3 330.2 %while.15 = (s32[]{:T(128)}, f32[768,2,128]{0,2,1:T(8,128)S(1)}, f32[2,128,17,128]{1,3,2,0:T(8,128)}, f32[768,128]{1,0:T(8,128)S(1)}, s32[]{:T(128)}) while((s32[]{:T(128)}, f32[768,2,128]{0,2,1:T(8,128)S(1)}, f32[2,128,17,128]{1,3,2,0:T(8,128)}, f32[768,128]{1,0:T(8,128)S(1)}, s32[]{:T(128)}) %tuple.40), condition=%wide.region_1.0_spmd, body=%wide.region_0.0_spmd.sunk | while | flops 301989888 | bytes 6029425 | solution.py:37
  11.3 14.4 %collective-permute-start = (f32[768,2,128]{0,2,1:T(8,128)S(1)}, f32[768,2,128]{0,2,1:T(8,128)S(1)}, u32[]{:S(2)}, u32[]{:S(2)}) collective-permute-start(f32[768,2,128]{0,2,1:T(8,128)S(1)} %copy.29), channel_id=1, source_target_pairs={{16,0},{32,16},{48,32},{64,48},{80,64},{96,80},{112,96},{128,112},... | collective-permute-start | bytes 2359304 | tf_op jit(solution)/shard_map/while/body/eval_jaxpr/ppermute | solution.py:10
  25.8 1.4 fusion.11
  27.2 14.7 %collective-permute-done = f32[768,2,128]{0,2,1:T(8,128)S(1)} collective-permute-done((f32[768,2,128]{0,2,1:T(8,128)S(1)}, f32[768,2,128]{0,2,1:T(8,128)S(1)}, u32[]{:S(2)}, u32[]{:S(2)}) %collective-permute-start) | collective-permute-done | bytes 786464 | tf_op jit(solution)/shard_map/while/body/eval_jaxpr/ppermute | solution.py:10
  42.0 7.7 %collective-permute-start = (f32[768,2,128]{0,2,1:T(8,128)S(1)}, f32[768,2,128]{0,2,1:T(8,128)S(1)}, u32[]{:S(2)}, u32[]{:S(2)}) collective-permute-start(f32[768,2,128]{0,2,1:T(8,128)S(1)} %copy.29), channel_id=1, source_target_pairs={{16,0},{32,16},{48,32},{64,48},{80,64},{96,80},{112,96},{128,112},... | collective-permute-start | bytes 2359304 | tf_op jit(solution)/shard_map/while/body/eval_jaxpr/ppermute | solution.py:10
  49.7 1.5 fusion.11
  51.2 13.8 %collective-permute-done = f32[768,2,128]{0,2,1:T(8,128)S(1)} collective-permute-done((f32[768,2,128]{0,2,1:T(8,128)S(1)}, f32[768,2,128]{0,2,1:T(8,128)S(1)}, u32[]{:S(2)}, u32[]{:S(2)}) %collective-permute-start) | collective-permute-done | bytes 786464 | tf_op jit(solution)/shard_map/while/body/eval_jaxpr/ppermute | solution.py:10
  65.0 7.7 %collective-permute-start = (f32[768,2,128]{0,2,1:T(8,128)S(1)}, f32[768,2,128]{0,2,1:T(8,128)S(1)}, u32[]{:S(2)}, u32[]{:S(2)}) collective-permute-start(f32[768,2,128]{0,2,1:T(8,128)S(1)} %copy.29), channel_id=1, source_target_pairs={{16,0},{32,16},{48,32},{64,48},{80,64},{96,80},{112,96},{128,112},... | collective-permute-start | bytes 2359304 | tf_op jit(solution)/shard_map/while/body/eval_jaxpr/ppermute | solution.py:10
  72.8 1.4 fusion.11
  74.2 12.9 %collective-permute-done = f32[768,2,128]{0,2,1:T(8,128)S(1)} collective-permute-done((f32[768,2,128]{0,2,1:T(8,128)S(1)}, f32[768,2,128]{0,2,1:T(8,128)S(1)}, u32[]{:S(2)}, u32[]{:S(2)}) %collective-permute-start) | collective-permute-done | bytes 786464 | tf_op jit(solution)/shard_map/while/body/eval_jaxpr/ppermute | solution.py:10
  87.2 7.7 %collective-permute-start = (f32[768,2,128]{0,2,1:T(8,128)S(1)}, f32[768,2,128]{0,2,1:T(8,128)S(1)}, u32[]{:S(2)}, u32[]{:S(2)}) collective-permute-start(f32[768,2,128]{0,2,1:T(8,128)S(1)} %copy.29), channel_id=1, source_target_pairs={{16,0},{32,16},{48,32},{64,48},{80,64},{96,80},{112,96},{128,112},... | collective-permute-start | bytes 2359304 | tf_op jit(solution)/shard_map/while/body/eval_jaxpr/ppermute | solution.py:10
  96.3 12.0 %collective-permute-done = f32[768,2,128]{0,2,1:T(8,128)S(1)} collective-permute-done((f32[768,2,128]{0,2,1:T(8,128)S(1)}, f32[768,2,128]{0,2,1:T(8,128)S(1)}, u32[]{:S(2)}, u32[]{:S(2)}) %collective-permute-start) | collective-permute-done | bytes 786464 | tf_op jit(solution)/shard_map/while/body/eval_jaxpr/ppermute | solution.py:10
  108.4 7.7 %collective-permute-start = (f32[768,2,128]{0,2,1:T(8,128)S(1)}, f32[768,2,128]{0,2,1:T(8,128)S(1)}, u32[]{:S(2)}, u32[]{:S(2)}) collective-permute-start(f32[768,2,128]{0,2,1:T(8,128)S(1)} %copy.29), channel_id=1, source_target_pairs={{16,0},{32,16},{48,32},{64,48},{80,64},{96,80},{112,96},{128,112},... | collective-permute-start | bytes 2359304 | tf_op jit(solution)/shard_map/while/body/eval_jaxpr/ppermute | solution.py:10
  117.5 11.1 %collective-permute-done = f32[768,2,128]{0,2,1:T(8,128)S(1)} collective-permute-done((f32[768,2,128]{0,2,1:T(8,128)S(1)}, f32[768,2,128]{0,2,1:T(8,128)S(1)}, u32[]{:S(2)}, u32[]{:S(2)}) %collective-permute-start) | collective-permute-done | bytes 786464 | tf_op jit(solution)/shard_map/while/body/eval_jaxpr/ppermute | solution.py:10
  128.7 7.7 %collective-permute-start = (f32[768,2,128]{0,2,1:T(8,128)S(1)}, f32[768,2,128]{0,2,1:T(8,128)S(1)}, u32[]{:S(2)}, u32[]{:S(2)}) collective-permute-start(f32[768,2,128]{0,2,1:T(8,128)S(1)} %copy.29), channel_id=1, source_target_pairs={{16,0},{32,16},{48,32},{64,48},{80,64},{96,80},{112,96},{128,112},... | collective-permute-start | bytes 2359304 | tf_op jit(solution)/shard_map/while/body/eval_jaxpr/ppermute | solution.py:10
  136.4 1.4 fusion.11
  137.8 10.1 %collective-permute-done = f32[768,2,128]{0,2,1:T(8,128)S(1)} collective-permute-done((f32[768,2,128]{0,2,1:T(8,128)S(1)}, f32[768,2,128]{0,2,1:T(8,128)S(1)}, u32[]{:S(2)}, u32[]{:S(2)}) %collective-permute-start) | collective-permute-done | bytes 786464 | tf_op jit(solution)/shard_map/while/body/eval_jaxpr/ppermute | solution.py:10
  148.0 7.7 %collective-permute-start = (f32[768,2,128]{0,2,1:T(8,128)S(1)}, f32[768,2,128]{0,2,1:T(8,128)S(1)}, u32[]{:S(2)}, u32[]{:S(2)}) collective-permute-start(f32[768,2,128]{0,2,1:T(8,128)S(1)} %copy.29), channel_id=1, source_target_pairs={{16,0},{32,16},{48,32},{64,48},{80,64},{96,80},{112,96},{128,112},... | collective-permute-start | bytes 2359304 | tf_op jit(solution)/shard_map/while/body/eval_jaxpr/ppermute | solution.py:10
  155.8 1.4 fusion.11
  157.2 9.2 %collective-permute-done = f32[768,2,128]{0,2,1:T(8,128)S(1)} collective-permute-done((f32[768,2,128]{0,2,1:T(8,128)S(1)}, f32[768,2,128]{0,2,1:T(8,128)S(1)}, u32[]{:S(2)}, u32[]{:S(2)}) %collective-permute-start) | collective-permute-done | bytes 786464 | tf_op jit(solution)/shard_map/while/body/eval_jaxpr/ppermute | solution.py:10
  166.5 7.7 %collective-permute-start = (f32[768,2,128]{0,2,1:T(8,128)S(1)}, f32[768,2,128]{0,2,1:T(8,128)S(1)}, u32[]{:S(2)}, u32[]{:S(2)}) collective-permute-start(f32[768,2,128]{0,2,1:T(8,128)S(1)} %copy.29), channel_id=1, source_target_pairs={{16,0},{32,16},{48,32},{64,48},{80,64},{96,80},{112,96},{128,112},... | collective-permute-start | bytes 2359304 | tf_op jit(solution)/shard_map/while/body/eval_jaxpr/ppermute | solution.py:10
  174.2 1.4 fusion.11
  175.6 8.3 %collective-permute-done = f32[768,2,128]{0,2,1:T(8,128)S(1)} collective-permute-done((f32[768,2,128]{0,2,1:T(8,128)S(1)}, f32[768,2,128]{0,2,1:T(8,128)S(1)}, u32[]{:S(2)}, u32[]{:S(2)}) %collective-permute-start) | collective-permute-done | bytes 786464 | tf_op jit(solution)/shard_map/while/body/eval_jaxpr/ppermute | solution.py:10
  184.0 7.7 %collective-permute-start = (f32[768,2,128]{0,2,1:T(8,128)S(1)}, f32[768,2,128]{0,2,1:T(8,128)S(1)}, u32[]{:S(2)}, u32[]{:S(2)}) collective-permute-start(f32[768,2,128]{0,2,1:T(8,128)S(1)} %copy.29), channel_id=1, source_target_pairs={{16,0},{32,16},{48,32},{64,48},{80,64},{96,80},{112,96},{128,112},... | collective-permute-start | bytes 2359304 | tf_op jit(solution)/shard_map/while/body/eval_jaxpr/ppermute | solution.py:10
  193.2 7.5 %collective-permute-done = f32[768,2,128]{0,2,1:T(8,128)S(1)} collective-permute-done((f32[768,2,128]{0,2,1:T(8,128)S(1)}, f32[768,2,128]{0,2,1:T(8,128)S(1)}, u32[]{:S(2)}, u32[]{:S(2)}) %collective-permute-start) | collective-permute-done | bytes 786464 | tf_op jit(solution)/shard_map/while/body/eval_jaxpr/ppermute | solution.py:10
  200.7 7.4 %collective-permute-start = (f32[768,2,128]{0,2,1:T(8,128)S(1)}, f32[768,2,128]{0,2,1:T(8,128)S(1)}, u32[]{:S(2)}, u32[]{:S(2)}) collective-permute-start(f32[768,2,128]{0,2,1:T(8,128)S(1)} %copy.29), channel_id=1, source_target_pairs={{16,0},{32,16},{48,32},{64,48},{80,64},{96,80},{112,96},{128,112},... | collective-permute-start | bytes 2359304 | tf_op jit(solution)/shard_map/while/body/eval_jaxpr/ppermute | solution.py:10
  208.1 1.4 fusion.11
  209.6 8.0 %collective-permute-done = f32[768,2,128]{0,2,1:T(8,128)S(1)} collective-permute-done((f32[768,2,128]{0,2,1:T(8,128)S(1)}, f32[768,2,128]{0,2,1:T(8,128)S(1)}, u32[]{:S(2)}, u32[]{:S(2)}) %collective-permute-start) | collective-permute-done | bytes 786464 | tf_op jit(solution)/shard_map/while/body/eval_jaxpr/ppermute | solution.py:10
  217.6 7.4 %collective-permute-start = (f32[768,2,128]{0,2,1:T(8,128)S(1)}, f32[768,2,128]{0,2,1:T(8,128)S(1)}, u32[]{:S(2)}, u32[]{:S(2)}) collective-permute-start(f32[768,2,128]{0,2,1:T(8,128)S(1)} %copy.29), channel_id=1, source_target_pairs={{16,0},{32,16},{48,32},{64,48},{80,64},{96,80},{112,96},{128,112},... | collective-permute-start | bytes 2359304 | tf_op jit(solution)/shard_map/while/body/eval_jaxpr/ppermute | solution.py:10
  225.0 1.4 fusion.11
  226.5 9.0 %collective-permute-done = f32[768,2,128]{0,2,1:T(8,128)S(1)} collective-permute-done((f32[768,2,128]{0,2,1:T(8,128)S(1)}, f32[768,2,128]{0,2,1:T(8,128)S(1)}, u32[]{:S(2)}, u32[]{:S(2)}) %collective-permute-start) | collective-permute-done | bytes 786464 | tf_op jit(solution)/shard_map/while/body/eval_jaxpr/ppermute | solution.py:10
  235.5 7.4 %collective-permute-start = (f32[768,2,128]{0,2,1:T(8,128)S(1)}, f32[768,2,128]{0,2,1:T(8,128)S(1)}, u32[]{:S(2)}, u32[]{:S(2)}) collective-permute-start(f32[768,2,128]{0,2,1:T(8,128)S(1)} %copy.29), channel_id=1, source_target_pairs={{16,0},{32,16},{48,32},{64,48},{80,64},{96,80},{112,96},{128,112},... | collective-permute-start | bytes 2359304 | tf_op jit(solution)/shard_map/while/body/eval_jaxpr/ppermute | solution.py:10
  244.4 10.1 %collective-permute-done = f32[768,2,128]{0,2,1:T(8,128)S(1)} collective-permute-done((f32[768,2,128]{0,2,1:T(8,128)S(1)}, f32[768,2,128]{0,2,1:T(8,128)S(1)}, u32[]{:S(2)}, u32[]{:S(2)}) %collective-permute-start) | collective-permute-done | bytes 786464 | tf_op jit(solution)/shard_map/while/body/eval_jaxpr/ppermute | solution.py:10
  254.6 7.4 %collective-permute-start = (f32[768,2,128]{0,2,1:T(8,128)S(1)}, f32[768,2,128]{0,2,1:T(8,128)S(1)}, u32[]{:S(2)}, u32[]{:S(2)}) collective-permute-start(f32[768,2,128]{0,2,1:T(8,128)S(1)} %copy.29), channel_id=1, source_target_pairs={{16,0},{32,16},{48,32},{64,48},{80,64},{96,80},{112,96},{128,112},... | collective-permute-start | bytes 2359304 | tf_op jit(solution)/shard_map/while/body/eval_jaxpr/ppermute | solution.py:10
  262.0 1.4 fusion.11
  263.5 11.2 %collective-permute-done = f32[768,2,128]{0,2,1:T(8,128)S(1)} collective-permute-done((f32[768,2,128]{0,2,1:T(8,128)S(1)}, f32[768,2,128]{0,2,1:T(8,128)S(1)}, u32[]{:S(2)}, u32[]{:S(2)}) %collective-permute-start) | collective-permute-done | bytes 786464 | tf_op jit(solution)/shard_map/while/body/eval_jaxpr/ppermute | solution.py:10
  274.7 7.4 %collective-permute-start = (f32[768,2,128]{0,2,1:T(8,128)S(1)}, f32[768,2,128]{0,2,1:T(8,128)S(1)}, u32[]{:S(2)}, u32[]{:S(2)}) collective-permute-start(f32[768,2,128]{0,2,1:T(8,128)S(1)} %copy.29), channel_id=1, source_target_pairs={{16,0},{32,16},{48,32},{64,48},{80,64},{96,80},{112,96},{128,112},... | collective-permute-start | bytes 2359304 | tf_op jit(solution)/shard_map/while/body/eval_jaxpr/ppermute | solution.py:10
  282.2 1.4 fusion.11
  283.6 12.3 %collective-permute-done = f32[768,2,128]{0,2,1:T(8,128)S(1)} collective-permute-done((f32[768,2,128]{0,2,1:T(8,128)S(1)}, f32[768,2,128]{0,2,1:T(8,128)S(1)}, u32[]{:S(2)}, u32[]{:S(2)}) %collective-permute-start) | collective-permute-done | bytes 786464 | tf_op jit(solution)/shard_map/while/body/eval_jaxpr/ppermute | solution.py:10
  295.9 7.4 %collective-permute-start = (f32[768,2,128]{0,2,1:T(8,128)S(1)}, f32[768,2,128]{0,2,1:T(8,128)S(1)}, u32[]{:S(2)}, u32[]{:S(2)}) collective-permute-start(f32[768,2,128]{0,2,1:T(8,128)S(1)} %copy.29), channel_id=1, source_target_pairs={{16,0},{32,16},{48,32},{64,48},{80,64},{96,80},{112,96},{128,112},... | collective-permute-start | bytes 2359304 | tf_op jit(solution)/shard_map/while/body/eval_jaxpr/ppermute | solution.py:10
  304.8 13.4 %collective-permute-done = f32[768,2,128]{0,2,1:T(8,128)S(1)} collective-permute-done((f32[768,2,128]{0,2,1:T(8,128)S(1)}, f32[768,2,128]{0,2,1:T(8,128)S(1)}, u32[]{:S(2)}, u32[]{:S(2)}) %collective-permute-start) | collective-permute-done | bytes 786464 | tf_op jit(solution)/shard_map/while/body/eval_jaxpr/ppermute | solution.py:10
  318.2 7.4 %collective-permute-start = (f32[768,2,128]{0,2,1:T(8,128)S(1)}, f32[768,2,128]{0,2,1:T(8,128)S(1)}, u32[]{:S(2)}, u32[]{:S(2)}) collective-permute-start(f32[768,2,128]{0,2,1:T(8,128)S(1)} %copy.29), channel_id=1, source_target_pairs={{16,0},{32,16},{48,32},{64,48},{80,64},{96,80},{112,96},{128,112},... | collective-permute-start | bytes 2359304 | tf_op jit(solution)/shard_map/while/body/eval_jaxpr/ppermute | solution.py:10
  325.6 1.4 fusion.11
  327.1 14.4 %collective-permute-done = f32[768,2,128]{0,2,1:T(8,128)S(1)} collective-permute-done((f32[768,2,128]{0,2,1:T(8,128)S(1)}, f32[768,2,128]{0,2,1:T(8,128)S(1)}, u32[]{:S(2)}, u32[]{:S(2)}) %collective-permute-start) | collective-permute-done | bytes 786464 | tf_op jit(solution)/shard_map/while/body/eval_jaxpr/ppermute | solution.py:10
  341.5 1.4 fusion.2
  343.0 4.8 copy.17
  349.7 148.8 %all-reduce.3.cloned.1.call-done = f32[2,128,2176]{2,0,1:T(2,128)} async-done(((f32[2,128,2176]{2,0,1:T(2,128)}), f32[2,128,2176]{2,0,1:T(2,128)}) %all-reduce.3.cloned.1.call-update) | async-done | bytes 2228240
  (31 shorter events, 13.5 us)
Async XLA Ops:
  7.2 491.4 %all-reduce.3.cloned.1.call-start = ((), (), s32[]{:S(2)}) async-start(), calls=%async_computation | async-start | bytes 4456448
  8.4 2.9 copy-start
  11.3 30.6 %collective-permute-start = (f32[768,2,128]{0,2,1:T(8,128)S(1)}, f32[768,2,128]{0,2,1:T(8,128)S(1)}, u32[]{:S(2)}, u32[]{:S(2)}) collective-permute-start(f32[768,2,128]{0,2,1:T(8,128)S(1)} %copy.29), channel_id=1, source_target_pairs={{16,0},{32,16},{48,32},{64,48},{80,64},{96,80},{112,96},{128,112},... | collective-permute-start | bytes 2359304 | tf_op jit(solution)/shard_map/while/body/eval_jaxpr/ppermute | solution.py:10
  42.0 23.0 %collective-permute-start = (f32[768,2,128]{0,2,1:T(8,128)S(1)}, f32[768,2,128]{0,2,1:T(8,128)S(1)}, u32[]{:S(2)}, u32[]{:S(2)}) collective-permute-start(f32[768,2,128]{0,2,1:T(8,128)S(1)} %copy.29), channel_id=1, source_target_pairs={{16,0},{32,16},{48,32},{64,48},{80,64},{96,80},{112,96},{128,112},... | collective-permute-start | bytes 2359304 | tf_op jit(solution)/shard_map/while/body/eval_jaxpr/ppermute | solution.py:10
  65.0 22.1 %collective-permute-start = (f32[768,2,128]{0,2,1:T(8,128)S(1)}, f32[768,2,128]{0,2,1:T(8,128)S(1)}, u32[]{:S(2)}, u32[]{:S(2)}) collective-permute-start(f32[768,2,128]{0,2,1:T(8,128)S(1)} %copy.29), channel_id=1, source_target_pairs={{16,0},{32,16},{48,32},{64,48},{80,64},{96,80},{112,96},{128,112},... | collective-permute-start | bytes 2359304 | tf_op jit(solution)/shard_map/while/body/eval_jaxpr/ppermute | solution.py:10
  87.2 21.2 %collective-permute-start = (f32[768,2,128]{0,2,1:T(8,128)S(1)}, f32[768,2,128]{0,2,1:T(8,128)S(1)}, u32[]{:S(2)}, u32[]{:S(2)}) collective-permute-start(f32[768,2,128]{0,2,1:T(8,128)S(1)} %copy.29), channel_id=1, source_target_pairs={{16,0},{32,16},{48,32},{64,48},{80,64},{96,80},{112,96},{128,112},... | collective-permute-start | bytes 2359304 | tf_op jit(solution)/shard_map/while/body/eval_jaxpr/ppermute | solution.py:10
  108.4 20.2 %collective-permute-start = (f32[768,2,128]{0,2,1:T(8,128)S(1)}, f32[768,2,128]{0,2,1:T(8,128)S(1)}, u32[]{:S(2)}, u32[]{:S(2)}) collective-permute-start(f32[768,2,128]{0,2,1:T(8,128)S(1)} %copy.29), channel_id=1, source_target_pairs={{16,0},{32,16},{48,32},{64,48},{80,64},{96,80},{112,96},{128,112},... | collective-permute-start | bytes 2359304 | tf_op jit(solution)/shard_map/while/body/eval_jaxpr/ppermute | solution.py:10
  128.7 19.3 %collective-permute-start = (f32[768,2,128]{0,2,1:T(8,128)S(1)}, f32[768,2,128]{0,2,1:T(8,128)S(1)}, u32[]{:S(2)}, u32[]{:S(2)}) collective-permute-start(f32[768,2,128]{0,2,1:T(8,128)S(1)} %copy.29), channel_id=1, source_target_pairs={{16,0},{32,16},{48,32},{64,48},{80,64},{96,80},{112,96},{128,112},... | collective-permute-start | bytes 2359304 | tf_op jit(solution)/shard_map/while/body/eval_jaxpr/ppermute | solution.py:10
  148.0 18.4 %collective-permute-start = (f32[768,2,128]{0,2,1:T(8,128)S(1)}, f32[768,2,128]{0,2,1:T(8,128)S(1)}, u32[]{:S(2)}, u32[]{:S(2)}) collective-permute-start(f32[768,2,128]{0,2,1:T(8,128)S(1)} %copy.29), channel_id=1, source_target_pairs={{16,0},{32,16},{48,32},{64,48},{80,64},{96,80},{112,96},{128,112},... | collective-permute-start | bytes 2359304 | tf_op jit(solution)/shard_map/while/body/eval_jaxpr/ppermute | solution.py:10
  166.5 17.5 %collective-permute-start = (f32[768,2,128]{0,2,1:T(8,128)S(1)}, f32[768,2,128]{0,2,1:T(8,128)S(1)}, u32[]{:S(2)}, u32[]{:S(2)}) collective-permute-start(f32[768,2,128]{0,2,1:T(8,128)S(1)} %copy.29), channel_id=1, source_target_pairs={{16,0},{32,16},{48,32},{64,48},{80,64},{96,80},{112,96},{128,112},... | collective-permute-start | bytes 2359304 | tf_op jit(solution)/shard_map/while/body/eval_jaxpr/ppermute | solution.py:10
  184.0 16.6 %collective-permute-start = (f32[768,2,128]{0,2,1:T(8,128)S(1)}, f32[768,2,128]{0,2,1:T(8,128)S(1)}, u32[]{:S(2)}, u32[]{:S(2)}) collective-permute-start(f32[768,2,128]{0,2,1:T(8,128)S(1)} %copy.29), channel_id=1, source_target_pairs={{16,0},{32,16},{48,32},{64,48},{80,64},{96,80},{112,96},{128,112},... | collective-permute-start | bytes 2359304 | tf_op jit(solution)/shard_map/while/body/eval_jaxpr/ppermute | solution.py:10
  200.7 16.8 %collective-permute-start = (f32[768,2,128]{0,2,1:T(8,128)S(1)}, f32[768,2,128]{0,2,1:T(8,128)S(1)}, u32[]{:S(2)}, u32[]{:S(2)}) collective-permute-start(f32[768,2,128]{0,2,1:T(8,128)S(1)} %copy.29), channel_id=1, source_target_pairs={{16,0},{32,16},{48,32},{64,48},{80,64},{96,80},{112,96},{128,112},... | collective-permute-start | bytes 2359304 | tf_op jit(solution)/shard_map/while/body/eval_jaxpr/ppermute | solution.py:10
  217.6 17.9 %collective-permute-start = (f32[768,2,128]{0,2,1:T(8,128)S(1)}, f32[768,2,128]{0,2,1:T(8,128)S(1)}, u32[]{:S(2)}, u32[]{:S(2)}) collective-permute-start(f32[768,2,128]{0,2,1:T(8,128)S(1)} %copy.29), channel_id=1, source_target_pairs={{16,0},{32,16},{48,32},{64,48},{80,64},{96,80},{112,96},{128,112},... | collective-permute-start | bytes 2359304 | tf_op jit(solution)/shard_map/while/body/eval_jaxpr/ppermute | solution.py:10
  235.5 19.0 %collective-permute-start = (f32[768,2,128]{0,2,1:T(8,128)S(1)}, f32[768,2,128]{0,2,1:T(8,128)S(1)}, u32[]{:S(2)}, u32[]{:S(2)}) collective-permute-start(f32[768,2,128]{0,2,1:T(8,128)S(1)} %copy.29), channel_id=1, source_target_pairs={{16,0},{32,16},{48,32},{64,48},{80,64},{96,80},{112,96},{128,112},... | collective-permute-start | bytes 2359304 | tf_op jit(solution)/shard_map/while/body/eval_jaxpr/ppermute | solution.py:10
  254.6 20.1 %collective-permute-start = (f32[768,2,128]{0,2,1:T(8,128)S(1)}, f32[768,2,128]{0,2,1:T(8,128)S(1)}, u32[]{:S(2)}, u32[]{:S(2)}) collective-permute-start(f32[768,2,128]{0,2,1:T(8,128)S(1)} %copy.29), channel_id=1, source_target_pairs={{16,0},{32,16},{48,32},{64,48},{80,64},{96,80},{112,96},{128,112},... | collective-permute-start | bytes 2359304 | tf_op jit(solution)/shard_map/while/body/eval_jaxpr/ppermute | solution.py:10
  274.7 21.2 %collective-permute-start = (f32[768,2,128]{0,2,1:T(8,128)S(1)}, f32[768,2,128]{0,2,1:T(8,128)S(1)}, u32[]{:S(2)}, u32[]{:S(2)}) collective-permute-start(f32[768,2,128]{0,2,1:T(8,128)S(1)} %copy.29), channel_id=1, source_target_pairs={{16,0},{32,16},{48,32},{64,48},{80,64},{96,80},{112,96},{128,112},... | collective-permute-start | bytes 2359304 | tf_op jit(solution)/shard_map/while/body/eval_jaxpr/ppermute | solution.py:10
  295.9 22.2 %collective-permute-start = (f32[768,2,128]{0,2,1:T(8,128)S(1)}, f32[768,2,128]{0,2,1:T(8,128)S(1)}, u32[]{:S(2)}, u32[]{:S(2)}) collective-permute-start(f32[768,2,128]{0,2,1:T(8,128)S(1)} %copy.29), channel_id=1, source_target_pairs={{16,0},{32,16},{48,32},{64,48},{80,64},{96,80},{112,96},{128,112},... | collective-permute-start | bytes 2359304 | tf_op jit(solution)/shard_map/while/body/eval_jaxpr/ppermute | solution.py:10
  318.2 23.3 %collective-permute-start = (f32[768,2,128]{0,2,1:T(8,128)S(1)}, f32[768,2,128]{0,2,1:T(8,128)S(1)}, u32[]{:S(2)}, u32[]{:S(2)}) collective-permute-start(f32[768,2,128]{0,2,1:T(8,128)S(1)} %copy.29), channel_id=1, source_target_pairs={{16,0},{32,16},{48,32},{64,48},{80,64},{96,80},{112,96},{128,112},... | collective-permute-start | bytes 2359304 | tf_op jit(solution)/shard_map/while/body/eval_jaxpr/ppermute | solution.py:10
Sparse Core Ops, SparseCore 0:
  347.9 150.5 all-reduce.2
where the time goes:
time: 508 us; the launch traced here: 507 us
  waiting for transfers between devices  327 us (64%)
  starting transfers between devices  128 us (25%)
  matrix products  24.4 us (5%)
  between operations  14.7 us (3%)
  local copies, waits for them, and re-layouts  12.7 us (2%)
    ppermute x16, waiting for transfers between devices, passed_along(): return lax.ppermute(block, axis, route)  178 us
    unnamed x2, waiting for transfers between devices  149 us
    ppermute x16, starting transfers between devices, passed_along(): return lax.ppermute(block, axis, route)  128 us
    dot_general x17, matrix products, pair_products(): jnp.einsum('pb,pmc->mbc', orbitals, shard_piece, precision=lax.Precision....  24.4 us
  transfers between devices with their start and end apart: 17, of which 17 were waited for; matrix products, arithmetic and copies ran while one was open for 5% of the time, Pallas kernels for 0%

commit v1 on v0

v1 whole, which is shorter than its diff:
```python
import functools

import jax
import jax.numpy as jnp
from jax import lax
from jax.experimental import pallas as pl
from jax.experimental.pallas import tpu as pltpu
from jax.sharding import PartitionSpec as P

MESH = pl.DeviceIdType.MESH
F32, BF16 = jnp.float32, jnp.bfloat16


def split(values):
    high = values.astype(BF16)
    return high, (values - high.astype(F32)).astype(BF16)


def dot(left, right):
    return jnp.dot(left, right, preferred_element_type=F32)


def kernel(
    bands, slabs, pieces, psi_ref, h_ref, margin_ref, hamilton_ref,
    block, high_w, low_w, total, core_in, core_sum, plane_in, result,
    ring_send, ring_recv, core_send, core_recv, plane_send, plane_recv, home_send, home_recv,
):
    half, groups = bands // 2, slabs // 2
    steps = half // 2
    width = psi_ref.shape[1]
    depth = psi_ref.shape[0] // pieces
    rows = width // slabs
    band, slab = lax.axis_index("band"), lax.axis_index("pw")
    core, group = lax.rem(slab, 2), lax.div(slab, 2)
    up = (lax.rem(band + 1, bands), slab)
    down = (lax.rem(band + bands - 1, bands), slab)
    across = (lax.rem(band + half, bands), slab)
    twin = (band, 2 * group + 1 - core)

    def plane_peer(distance):
        return (band, 2 * lax.rem(group + distance, groups) + core)

    barrier = pltpu.get_barrier_semaphore()
    partners = [up, down, across, twin] + [plane_peer(d) for d in range(1, groups)]
    for partner in partners:
        pl.semaphore_signal(barrier, inc=1, device_id=partner, device_id_type=MESH)

    for j in range(pieces):
        turned = psi_ref[pl.ds(j * depth, depth), :].T
        for g in range(groups):
            for c in range(2):
                block[0, j, pl.ds((c * groups + g) * rows, rows), :] = turned[(2 * g + c) * rows : (2 * g + c + 1) * rows, :]
    pl.semaphore_wait(barrier, len(partners))

    def ring(source, target, j, send, device):
        return pltpu.make_async_remote_copy(
            src_ref=block.at[source, j], dst_ref=block.at[target, j], send_sem=ring_send.at[send, j],
            recv_sem=ring_recv.at[target, j], device_id=device, device_id_type=MESH,
        )

    def go_up(k, j):
        return ring(k, k + 1, j, k, up)

    def go_down(k, j):
        return ring(k, k - 1, j, k, down)

    def go_across(j):
        return ring(0, half, j, steps, across)

    for j in range(pieces):
        go_up(0, j).start()
        go_across(j).start()

    for j in range(pieces):
        for ref, lanes in ((psi_ref, slice(0, width)), (h_ref, slice(width, 2 * width))):
            high, low = split(ref[pl.ds(j * depth, depth), :])
            high_w[j, :, lanes] = high
            low_w[j, :, lanes] = low

    def multiply(s, slots, j):
        highs, lows = zip(*[split(block[k, j]) for k in slots])
        n = len(slots)
        upper = dot(jnp.concatenate(highs + lows, axis=0), high_w[j])
        lower = dot(jnp.concatenate(highs, axis=0), low_w[j])
        for i in range(n):
            part = (
                upper[i * width : (i + 1) * width]
                + (upper[(n + i) * width : (n + i + 1) * width] + lower[i * width : (i + 1) * width])
            )
            if j == 0:
                total[s, i] = part
            else:
                total[s, i] += part

    def core_copy(s, n):
        theirs = pl.ds(pl.multiple_of((1 - core) * (width // 2), width // 2), width // 2)
        return pltpu.make_async_remote_copy(
            src_ref=total.at[s, pl.ds(0, n), theirs], dst_ref=core_in.at[s, pl.ds(0, n)],
            send_sem=core_send.at[s], recv_sem=core_recv.at[s], device_id=twin, device_id_type=MESH,
        )

    def plane_copy(s, n, distance):
        peer = lax.rem(group + distance, groups)
        theirs = pl.ds(pl.multiple_of(peer * rows, rows), rows)
        return pltpu.make_async_remote_copy(
            src_ref=core_sum.at[s, pl.ds(0, n), theirs], dst_ref=plane_in.at[s, distance - 1, pl.ds(0, n)],
            send_sem=plane_send.at[s], recv_sem=plane_recv.at[s],
            device_id=plane_peer(distance), device_id_type=MESH,
        )

    def plane_all(s, n):
        everything = plane_in.at[s, :, pl.ds(0, n)]
        return pltpu.make_async_remote_copy(
            src_ref=everything, dst_ref=everything, send_sem=plane_send.at[s], recv_sem=plane_recv.at[s],
            device_id=plane_peer(1), device_id_type=MESH,
        )

    def home_copy(s, i, k, which):
        out = (margin_ref, hamilton_ref)[which]
        there = pl.ds(pl.multiple_of(k * width, width), width)
        return pltpu.make_async_remote_copy(
            src_ref=result.at[s, i, :, pl.ds(which * width, width)], dst_ref=out.at[:, there],
            send_sem=home_send.at[k, which], recv_sem=home_recv.at[k, which],
            device_id=(lax.rem(band + bands - k, bands), slab), device_id_type=MESH,
        )

    def to_twin(s, n):
        core_copy(s, n).start()

    def to_plane(s, n):
        core_copy(s, n).wait_recv()
        mine = pl.ds(pl.multiple_of(core * (width // 2), width // 2), width // 2)
        for i in range(n):
            core_sum[s, i] = total[s, i, mine, :] + core_in[s, i]
        for d in range(1, groups):
            plane_copy(s, n, d).start()

    def summed(s, i):
        value = core_sum[s, i, pl.ds(pl.multiple_of(group * rows, rows), rows), :]
        for d in range(1, groups):
            value = value + plane_in[s, d - 1, i]
        return value

    def to_home(s):
        plane_all(s, 2).wait_recv()
        for i, k in enumerate((s, half + 1 - s)):
            result[s, i] = summed(s, i)
            for which in range(2):
                home_copy(s, i, k, which).start()

    for j in range(pieces):
        multiply(0, (0,), j)
    to_twin(0, 1)

    def step(s, _):
        other = half + 1 - s
        for j in range(pieces):
            go_up(s - 1, j).wait_recv()

            @pl.when(s < steps)
            def _():
                go_up(s, j).start()

            ring(0, other, j, 0, up).wait_recv()

            @pl.when(s < steps)
            def _():
                go_down(other, j).start()

            multiply(s, (s, other), j)
            if j == 0:
                @pl.when(s > 1)
                def _():
                    to_plane(s - 1, 2)
            if j == 1:
                @pl.when(s > 2)
                def _():
                    to_home(s - 2)
            if j == 2:
                @pl.when(s == 1)
                def _():
                    to_plane(0, 1)
        to_twin(s, 2)
        return 0

    lax.fori_loop(1, steps + 1, step, 0)
    to_plane(steps, 2)
    to_home(steps - 1)
    plane_all(0, 1).wait_recv()
    own = summed(0, 0)
    margin_ref[:, pl.ds(0, width)] = own[:, :width]
    hamilton_ref[:, pl.ds(0, width)] = own[:, width:]
    to_home(steps)

    def ring_sent(k, _):
        for j in range(pieces):
            ring(k, 0, j, k, up).wait_send()
        return 0

    lax.fori_loop(0, steps + 1, ring_sent, 0)
    lax.fori_loop(steps + 2, half + 1, ring_sent, 0)
    core_copy(0, 1).wait_send()
    plane_all(0, 1).wait_send()

    def sums_sent(s, _):
        core_copy(s, 2).wait_send()
        plane_all(s, 2).wait_send()
        return 0

    lax.fori_loop(1, steps + 1, sums_sent, 0)

    def home_done(k, _):
        for which in range(2):
            home_copy(0, 0, k, which).wait()
        return 0

    lax.fori_loop(1, half + 1, home_done, 0)


def solution(mesh):
    bands, slabs = mesh.shape["band"], mesh.shape["pw"]
    half, groups = bands // 2, slabs // 2
    steps = half // 2
    pieces = 3

    def shards(psi, h):
        depth, width = psi.shape
        rows = width // slabs
        out = jax.ShapeDtypeStruct((rows, (half + 1) * width), F32)
        vmem = pl.BlockSpec(memory_space=pltpu.VMEM)
        dma = pltpu.SemaphoreType.DMA
        return pl.pallas_call(
            functools.partial(kernel, bands, slabs, pieces),
            out_shape=(out, out),
            in_specs=[vmem, vmem],
            out_specs=(vmem, vmem),
            scratch_shapes=[
                pltpu.VMEM((half + 1, pieces, width, depth // pieces), F32),
                pltpu.VMEM((pieces, depth // pieces, 2 * width), BF16),
                pltpu.VMEM((pieces, depth // pieces, 2 * width), BF16),
                pltpu.VMEM((steps + 1, 2, width, 2 * width), F32),
                pltpu.VMEM((steps + 1, 2, width // 2, 2 * width), F32),
                pltpu.VMEM((steps + 1, 2, width // 2, 2 * width), F32),
                pltpu.VMEM((steps + 1, groups - 1, 2, rows, 2 * width), F32),
                pltpu.VMEM((steps + 1, 2, rows, 2 * width), F32),
                dma((half + 1, pieces)),
                dma((half + 1, pieces)),
                dma((steps + 1,)),
                dma((steps + 1,)),
                dma((steps + 1,)),
                dma((steps + 1,)),
                dma((half + 1, 2)),
                dma((half + 1, 2)),
            ],
            compiler_params=pltpu.CompilerParams(
                collective_id=0, has_side_effects=True, vmem_limit_bytes=40 << 20
            ),
            cost_estimate=pl.CostEstimate(
                flops=6 * (half + 1) * depth * width * 2 * width,
                bytes_accessed=4 * (2 * depth * width + 2 * rows * (half + 1) * width),
                transcendentals=0,
            ),
        )(psi, h)

    return jax.shard_map(
        shards,
        mesh=mesh,
        in_specs=(P("pw", "band"), P("pw", "band")),
        out_specs=(P(("band", "pw"), None), P(("band", "pw"), None)),
        check_vma=False,
    )
```

time: 508 us -> 133 us (0.26)
  waiting for transfers between devices: 327 us -> 0 us
  Pallas kernels: 0 us -> 129 us
  starting transfers between devices: 128 us -> 0 us
  matrix products: 24.4 us -> 0 us
  between operations: 14.7 us -> 0.65 us
  local copies, waits for them, and re-layouts: 12.7 us -> 3.25 us
    ppermute x16 -> x0, waiting for transfers between devices: 178 us -> none  [passed_along(): return lax.ppermute(block, axis, route)]
    unnamed x2 -> x0, waiting for transfers between devices: 149 us -> none
    pallas_call x0 -> x1, Pallas kernels: none -> 129 us  [shards(): pl.pallas_call(functools.partial(kernel, bands, slabs, pieces), out_shape...]
    ppermute x16 -> x0, starting transfers between devices: 128 us -> none  [passed_along(): return lax.ppermute(block, axis, route)]
    dot_general x17 -> x0, matrix products: 24.4 us -> none  [pair_products(): jnp.einsum('pb,pmc->mbc', orbitals, shard_piece, precision=lax.Precision....]
  transfers between devices with their start and end apart: 17 -> 0, of which waited for: 17 -> 0; matrix products, arithmetic and copies ran while one was open for 5% -> 0% of each run, Pallas kernels for 0% -> 0%
where the time goes in v1:
time: 133 us
  Pallas kernels  129 us (97%)
  local copies, waits for them, and re-layouts  3.25 us (2%)
    pallas_call x1, Pallas kernels, shards(): pl.pallas_call(functools.partial(kernel, bands, slabs, pieces), out_shape...  129 us
    unnamed x6, local copies, waits for them, and re-layouts  3.25 us

profile of v1, /device:TPU:1, one launch (start us, length us, event | category | flops | bytes accessed | tf_op | source)
XLA Modules:
  0.0 132.8 jit_solution(18444771093162826761)
XLA Ops:
  0.6 0.0 copy-start
  0.6 1.0 copy-done
  1.6 0.0 copy-start.1
  1.6 1.0 copy-done.1
  2.6 128.9 %shard_map.41 = (f32[8,2176]{1,0:T(8,128)S(1)}, f32[8,2176]{1,0:T(8,128)S(1)}) custom-call(f32[768,128]{1,0:T(8,128)S(1)} %copy-done, f32[768,128]{1,0:T(8,128)S(1)} %copy-done.1), custom_call_target="tpu_custom_call" | custom-call | flops 2566914048 | bytes 925696 | tf_op jit(solution)/shard_map/pallas_call | solution.py:232
  131.5 0.6 copy.6
  132.1 0.6 copy.7
Async XLA Ops:
  0.6 1.0 copy-start
  1.6 1.0 copy-start.1

commit v2 on v0

v2 whole, which is shorter than its diff:
```python
import functools

import jax
import jax.numpy as jnp
from jax import lax
from jax.experimental import pallas as pl
from jax.experimental.pallas import tpu as pltpu
from jax.sharding import PartitionSpec as P

MESH = pl.DeviceIdType.MESH
F32, BF16 = jnp.float32, jnp.bfloat16


def split(values):
    high = values.astype(BF16)
    return high, (values - high.astype(F32)).astype(BF16)


def kernel(
    bands, slabs, psi_hbm, h_hbm, margin_ref, hamilton_ref,
    psi, h, turned_away, image, block, weight, total, core_in, core_sum, plane_in, result,
    load_sem, ring_send, ring_recv, across_send, across_recv, image_send, image_recv,
    core_send, core_recv, plane_send, plane_recv, home_send, home_recv,
):
    planes, groups = bands // 2, slabs // 2
    last = planes // 2
    depth, width = psi.shape[0] // 2, psi.shape[1]
    half = width // 2
    rows = width // slabs
    band, slab = lax.axis_index("band"), lax.axis_index("pw")
    side, plane = lax.div(band, planes), lax.rem(band, planes)
    group, core = lax.div(slab, 2), lax.rem(slab, 2)

    def at_plane(distance):
        return (side * planes + lax.rem(plane + distance + planes, planes), slab)

    def plane_peer(distance):
        there = lax.rem(side + distance // groups, 2)
        return (there * planes + plane, 2 * lax.rem(group + distance % groups, groups) + core)

    up, down, across = at_plane(1), at_plane(-1), plane_peer(groups)
    twin = (band, 2 * group + 1 - core)

    def load(i):
        return pltpu.make_async_copy((psi_hbm, h_hbm)[i], (psi, h)[i], load_sem.at[i])

    load(0).start()
    load(1).start()
    barrier = pltpu.get_barrier_semaphore()
    partners = [up, down, twin] + [plane_peer(d) for d in range(1, 2 * groups)]
    for partner in partners:
        pl.semaphore_signal(barrier, inc=1, device_id=partner, device_id_type=MESH)

    mine = pl.ds(pl.multiple_of(side * depth, depth), depth)
    theirs = pl.ds(pl.multiple_of((1 - side) * depth, depth), depth)

    def turn(part, ref, lead):
        turned = psi[part, :].T
        for c in range(2):
            for g in range(groups):
                place = (2 * g + c) * rows
                ref[lead + (c, pl.ds(g * rows, rows), slice(None))] = turned[place : place + rows, :]

    load(0).wait()
    turn(mine, block, (0, 0))
    turn(theirs, turned_away, ())
    load(1).wait()
    pl.semaphore_wait(barrier, len(partners))

    def ring(source, target, o, r, send, device):
        return pltpu.make_async_remote_copy(
            src_ref=block.at[source, o, r], dst_ref=block.at[target, o, r], send_sem=ring_send.at[send, o, r],
            recv_sem=ring_recv.at[target, o, r], device_id=device, device_id_type=MESH,
        )

    def go_up(s, o, r):
        return ring(s, s + 1, o, r, s, up)

    def go_down(s, o, r):
        source = 0 if isinstance(s, int) and s == 0 else last + s
        return ring(source, last + s + 1, o, r, last + s, down)

    def hand_across(r):
        return pltpu.make_async_remote_copy(
            src_ref=turned_away.at[r], dst_ref=block.at[0, 1, r], send_sem=across_send.at[r],
            recv_sem=across_recv.at[r], device_id=across, device_id_type=MESH,
        )

    def hand_image(i):
        return pltpu.make_async_remote_copy(
            src_ref=(psi, h)[i].at[theirs], dst_ref=image.at[i], send_sem=image_send.at[i],
            recv_sem=image_recv.at[i], device_id=across, device_id_type=MESH,
        )

    for r in range(2):
        go_up(0, 0, r).start()
        go_down(0, 0, r).start()
        hand_across(r).start()
    for i in range(2):
        hand_image(i).start()

    def weigh(o, values, lanes):
        high, low = split(values)
        weight[o, pl.ds(0, depth), lanes] = high
        weight[o, pl.ds(depth, depth), lanes] = low
        weight[o, pl.ds(2 * depth, depth), lanes] = high

    weigh(0, psi[mine, :], slice(0, width))
    weigh(0, h[mine, :], slice(width, 2 * width))
    for r in range(2):
        hand_across(r).wait_recv()
        go_up(0, 1, r).start()
        go_down(0, 1, r).start()

    def left(n, o):
        values = jnp.concatenate([block[n, o, 0], block[n, o, 1]], axis=0)
        high, low = split(values)
        return jnp.concatenate([high, high, low], axis=1)

    def multiply(s, sources):
        for o in range(2):
            ours = [lax.rem(o + turn_over, 2) for _, turn_over in sources]
            lefts = [left(n(w), w) for w, (n, _) in zip(ours, sources)]
            product = jnp.dot(jnp.concatenate(lefts, axis=0), weight[o], preferred_element_type=F32)
            for u, w in enumerate(ours):
                total[s, u, w] = product[u * width : (u + 1) * width]

    def multiply_pair(s):
        above = jnp.where(s == 0, 0, last + s)
        multiply(s, (
            (lambda o: s, jnp.where(plane < s, 1, 0)),
            (lambda o: above, jnp.where(plane + s < planes, 1, 0)),
        ))

    def multiply_last():
        multiply(last, ((lambda o: last * (1 + o), jnp.where(plane < last, 1, 0)),))

    def core_copy(s, n):
        return pltpu.make_async_remote_copy(
            src_ref=total.at[s, pl.ds(0, n), :, pl.ds(pl.multiple_of((1 - core) * half, half), half)],
            dst_ref=core_in.at[s, pl.ds(0, n)],
            send_sem=core_send.at[s], recv_sem=core_recv.at[s], device_id=twin, device_id_type=MESH,
        )

    def plane_copy(s, n, distance):
        there = lax.rem(group + distance % groups, groups)
        return pltpu.make_async_remote_copy(
            src_ref=core_sum.at[s, pl.ds(0, n), distance // groups, pl.ds(pl.multiple_of(there * rows, rows), rows)],
            dst_ref=plane_in.at[s, distance - 1, pl.ds(0, n)],
            send_sem=plane_send.at[s], recv_sem=plane_recv.at[s],
            device_id=plane_peer(distance), device_id_type=MESH,
        )

    def plane_all(s, n):
        everything = plane_in.at[s, :, pl.ds(0, n)]
        return pltpu.make_async_remote_copy(
            src_ref=everything, dst_ref=everything, send_sem=plane_send.at[s], recv_sem=plane_recv.at[s],
            device_id=across, device_id_type=MESH,
        )

    def home_copy(s, u, k, which, device):
        out = (margin_ref, hamilton_ref)[which]
        return pltpu.make_async_remote_copy(
            src_ref=result.at[s, u, :, pl.ds(which * width, width)],
            dst_ref=out.at[:, pl.ds(pl.multiple_of(k * width, width), width)],
            send_sem=home_send.at[k, which], recv_sem=home_recv.at[k, which], device_id=device, device_id_type=MESH,
        )

    def to_twin(s, n):
        core_copy(s, n).start()

    def to_plane(s, n):
        core_copy(s, n).wait_recv()
        ours = pl.ds(pl.multiple_of(core * half, half), half)
        for u in range(n):
            for o in range(2):
                core_sum[s, u, o] = total[s, u, o, ours, :] + core_in[s, u, o]
        for d in range(1, 2 * groups):
            plane_copy(s, n, d).start()

    def summed(s, u):
        value = core_sum[s, u, 0, pl.ds(pl.multiple_of(group * rows, rows), rows), :]
        for d in range(1, 2 * groups):
            value = value + plane_in[s, d - 1, u]
        return value

    def to_home(s, n):
        plane_all(s, n).wait_recv()
        for u in range(n):
            result[s, u] = summed(s, u)
            for which in range(2):
                home_copy(s, u, planes - s if u else s, which, at_plane(s if u else -s)).start()

    def stay_home():
        plane_all(0, 2).wait_recv()
        for u, k in ((0, 0), (1, planes)):
            value = summed(0, u)
            margin_ref[:, pl.ds(k * width, width)] = value[:, :width]
            hamilton_ref[:, pl.ds(k * width, width)] = value[:, width:]

    def step(s, _):
        for o in range(2):
            for r in range(2):
                go_up(s - 1, o, r).wait_recv()
                if o == 0:
                    go_up(s, o, r).start()
                else:
                    pl.when(s < last - 1)(lambda: go_up(s, o, r).start())
                ring(0, last + s, o, r, 0, down).wait_recv()
                if o == 1:
                    go_down(s, o, r).start()
                else:
                    pl.when(s < last - 1)(lambda: go_down(s, o, r).start())
                if (o, r) == (0, 0):
                    pl.when(s > 1)(lambda: to_plane(s - 2, 2))
                if (o, r) == (0, 1):
                    pl.when(s > 3)(lambda: to_home(s - 3, 2))

        @pl.when(s == 1)
        def _():
            for i in range(2):
                hand_image(i).wait_recv()
                weigh(1, image[i], slice(i * width, (i + 1) * width))

        multiply_pair(s - 1)
        to_twin(s - 1, 2)
        return 0

    lax.fori_loop(1, last, step, 0)
    multiply_pair(last - 1)
    to_twin(last - 1, 2)
    to_plane(last - 2, 2)
    to_home(last - 3, 2)
    for r in range(2):
        go_up(last - 1, 0, r).wait_recv()
        ring(0, 2 * last, 1, r, 0, down).wait_recv()
    multiply_last()
    to_twin(last, 1)
    to_plane(last - 1, 2)
    to_plane(last, 1)
    to_home(last - 2, 2)
    stay_home()
    to_home(last - 1, 2)
    to_home(last, 1)

    def ring_sent(s, _):
        for o in range(2):
            for r in range(2):
                ring(0, 1, o, r, s, up).wait_send()
        return 0

    lax.fori_loop(0, last - 1, ring_sent, 0)
    lax.fori_loop(last, 2 * last - 1, ring_sent, 0)
    for r in range(2):
        ring(0, 1, 0, r, last - 1, up).wait_send()
        ring(0, 1, 1, r, 2 * last - 1, up).wait_send()
        hand_across(r).wait_send()
        hand_image(r).wait_send()

    def sums_sent(s, _):
        core_copy(s, 2).wait_send()
        plane_all(s, 2).wait_send()
        return 0

    lax.fori_loop(0, last, sums_sent, 0)
    core_copy(last, 1).wait_send()
    plane_all(last, 1).wait_send()

    def home_done(k, _):
        for which in range(2):
            home_copy(0, 0, k, which, up).wait()
        return 0

    lax.fori_loop(1, planes, home_done, 0)


def solution(mesh):
    bands, slabs = mesh.shape["band"], mesh.shape["pw"]
    planes, groups = bands // 2, slabs // 2
    last = planes // 2

    def shards(psi, h):
        depth, width = psi.shape[0] // 2, psi.shape[1]
        half, rows = width // 2, width // slabs
        out = jax.ShapeDtypeStruct((rows, (planes + 1) * width), F32)
        vmem, anywhere = pl.BlockSpec(memory_space=pltpu.VMEM), pl.BlockSpec(memory_space=pl.ANY)
        dma = pltpu.SemaphoreType.DMA
        return pl.pallas_call(
            functools.partial(kernel, bands, slabs),
            out_shape=(out, out),
            in_specs=[anywhere, anywhere],
            out_specs=(vmem, vmem),
            scratch_shapes=[
                pltpu.VMEM(psi.shape, F32),
                pltpu.VMEM(h.shape, F32),
                pltpu.VMEM((2, half, depth), F32),
                pltpu.VMEM((2, depth, width), F32),
                pltpu.VMEM((planes + 1, 2, 2, half, depth), F32),
                pltpu.VMEM((2, 3 * depth, 2 * width), BF16),
                pltpu.VMEM((last + 1, 2, 2, width, 2 * width), F32),
                pltpu.VMEM((last + 1, 2, 2, half, 2 * width), F32),
                pltpu.VMEM((last + 1, 2, 2, half, 2 * width), F32),
                pltpu.VMEM((last + 1, 2 * groups - 1, 2, rows, 2 * width), F32),
                pltpu.VMEM((last + 1, 2, rows, 2 * width), F32),
                dma((2,)),
                dma((planes, 2, 2)),
                dma((planes + 1, 2, 2)),
                dma((2,)),
                dma((2,)),
                dma((2,)),
                dma((2,)),
                dma((last + 1,)),
                dma((last + 1,)),
                dma((last + 1,)),
                dma((last + 1,)),
                dma((planes, 2)),
                dma((planes, 2)),
            ],
            compiler_params=pltpu.CompilerParams(
                collective_id=0, has_side_effects=True, vmem_limit_bytes=48 << 20
            ),
            cost_estimate=pl.CostEstimate(
                flops=6 * (planes + 1) * 2 * depth * width * 2 * width,
                bytes_accessed=4 * (4 * depth * width + 2 * rows * (planes + 1) * width),
                transcendentals=0,
            ),
        )(psi, h)

    return jax.shard_map(
        shards,
        mesh=mesh,
        in_specs=(P("pw", "band"), P("pw", "band")),
        out_specs=(P(("band", "pw"), None), P(("band", "pw"), None)),
        check_vma=False,
    )
```

time: 508 us -> 105 us (0.21)
  waiting for transfers between devices: 327 us -> 0 us
  starting transfers between devices: 128 us -> 0 us
  Pallas kernels: 0 us -> 101 us
  matrix products: 24.4 us -> 0 us
  between operations: 14.7 us -> 0.65 us
  local copies, waits for them, and re-layouts: 12.7 us -> 3.25 us
    ppermute x16 -> x0, waiting for transfers between devices: 178 us -> none  [passed_along(): return lax.ppermute(block, axis, route)]
    unnamed x2 -> x0, waiting for transfers between devices: 149 us -> none
    ppermute x16 -> x0, starting transfers between devices: 128 us -> none  [passed_along(): return lax.ppermute(block, axis, route)]
    pallas_call x0 -> x1, Pallas kernels: none -> 101 us  [shards(): pl.pallas_call(functools.partial(kernel, bands, slabs), out_shape=(out, o...]
    dot_general x17 -> x0, matrix products: 24.4 us -> none  [pair_products(): jnp.einsum('pb,pmc->mbc', orbitals, shard_piece, precision=lax.Precision....]
  transfers between devices with their start and end apart: 17 -> 0, of which waited for: 17 -> 0; matrix products, arithmetic and copies ran while one was open for 5% -> 0% of each run, Pallas kernels for 0% -> 0%
where the time goes in v2:
time: 105 us; the launch traced here: 104 us
  Pallas kernels  101 us (96%)
  local copies, waits for them, and re-layouts  3.25 us (3%)
    pallas_call x1, Pallas kernels, shards(): pl.pallas_call(functools.partial(kernel, bands, slabs), out_shape=(out, o...  101 us
    unnamed x6, local copies, waits for them, and re-layouts  3.25 us

profile of v2, /device:TPU:1, one launch (start us, length us, event | category | flops | bytes accessed | tf_op | source)
XLA Modules:
  0.0 104.4 jit_solution(9241347367875006479)
XLA Ops:
  0.6 0.0 copy-start
  0.6 1.0 copy-done
  1.6 0.0 copy-start.1
  1.6 1.0 copy-done.1
  2.6 100.5 %shard_map.41 = (f32[8,2176]{1,0:T(8,128)S(1)}, f32[8,2176]{1,0:T(8,128)S(1)}) custom-call(f32[768,128]{1,0:T(8,128)S(1)} %copy-done, f32[768,128]{1,0:T(8,128)S(1)} %copy-done.1), custom_call_target="tpu_custom_call" | custom-call | flops 2566914048 | bytes 925696 | tf_op jit(solution)/shard_map/pallas_call | solution.py:288
  103.2 0.6 copy.6
  103.8 0.6 copy.7
Async XLA Ops:
  0.6 1.0 copy-start
  1.6 1.0 copy-start.1

commit v3 on v2

v3 whole, which is shorter than its diff:
```python
import functools

import jax
import jax.numpy as jnp
from jax import lax
from jax.experimental import pallas as pl
from jax.experimental.pallas import tpu as pltpu
from jax.sharding import PartitionSpec as P

MESH = pl.DeviceIdType.MESH
F32, BF16 = jnp.float32, jnp.bfloat16


def split(values):
    high = values.astype(BF16)
    return high, (values - high.astype(F32)).astype(BF16)


def kernel(
    bands, slabs, psi_hbm, h_hbm, margin_ref, hamilton_ref,
    psi, h, turned_away, image, block, weight, total, core_in, core_sum, plane_in, result,
    load_sem, ring_send, ring_recv, across_send, across_recv, image_send, image_recv,
    core_send, core_recv, plane_send, plane_recv, home_send, home_recv,
):
    planes, groups = bands // 2, slabs // 2
    pairs = planes // 2
    parts = block.shape[3]
    depth, width = psi.shape[0] // 2, psi.shape[1]
    half = width // 2
    rows = width // slabs
    band, slab = lax.axis_index("band"), lax.axis_index("pw")
    side, plane = lax.div(band, planes), lax.rem(band, planes)
    group, core = lax.div(slab, 2), lax.rem(slab, 2)

    def at_plane(distance):
        return (side * planes + lax.rem(plane + distance + planes, planes), slab)

    def plane_peer(distance):
        there = lax.rem(side + distance // groups, 2)
        return (there * planes + plane, 2 * lax.rem(group + distance % groups, groups) + core)

    up, down, across = at_plane(1), at_plane(-1), plane_peer(groups)
    twin = (band, 2 * group + 1 - core)

    def load(i):
        return pltpu.make_async_copy((psi_hbm, h_hbm)[i], (psi, h)[i], load_sem.at[i])

    load(0).start()
    load(1).start()
    barrier = pltpu.get_barrier_semaphore()
    partners = [up, down, twin] + [plane_peer(d) for d in range(1, 2 * groups)]
    for partner in partners:
        pl.semaphore_signal(barrier, inc=1, device_id=partner, device_id_type=MESH)

    mine = pl.ds(pl.multiple_of(side * depth, depth), depth)
    theirs = pl.ds(pl.multiple_of((1 - side) * depth, depth), depth)

    def turn(part, ref, lead):
        turned = psi[part, :].T
        for c in range(2):
            for g in range(groups):
                place = (2 * g + c) * rows
                piece, row = divmod(g * rows, half // parts)
                ref[lead(c, piece) + (pl.ds(row, rows), slice(None))] = turned[place : place + rows, :]

    load(0).wait()
    turn(mine, block, lambda c, piece: (0, c, 0, piece))
    turn(theirs, turned_away, lambda c, piece: (c, piece))
    load(1).wait()
    pl.semaphore_wait(barrier, len(partners))

    def ring(s, r, o, j):
        return pltpu.make_async_remote_copy(
            src_ref=block.at[s, r, o, j], dst_ref=block.at[s + 1, r, o, j], send_sem=ring_send.at[s, r, o, j],
            recv_sem=ring_recv.at[s + 1, r, o, j], device_id=(up, down)[r], device_id_type=MESH,
        )

    def hand_across(r, j):
        return pltpu.make_async_remote_copy(
            src_ref=turned_away.at[r, j], dst_ref=block.at[0, r, 1, j], send_sem=across_send.at[r, j],
            recv_sem=across_recv.at[r, j], device_id=across, device_id_type=MESH,
        )

    def hand_image(i):
        return pltpu.make_async_remote_copy(
            src_ref=(psi, h)[i].at[theirs], dst_ref=image.at[i], send_sem=image_send.at[i],
            recv_sem=image_recv.at[i], device_id=across, device_id_type=MESH,
        )

    for j in range(parts):
        for r in range(2):
            ring(0, r, 0, j).start()
            hand_across(r, j).start()
    for i in range(2):
        hand_image(i).start()

    def weigh(o, values, lanes):
        high, low = split(values)
        weight[o, pl.ds(0, depth), lanes] = high
        weight[o, pl.ds(depth, depth), lanes] = low
        weight[o, pl.ds(2 * depth, depth), lanes] = high

    weigh(0, psi[mine, :], slice(0, width))
    weigh(0, h[mine, :], slice(width, 2 * width))

    def pass_on(s, o, j):
        for r in range(2):
            ring(s - 1, r, o, j).wait_recv()
            ring(s, r, o, j).start()

    def left(s, r, o):
        high, low = split(block[s, r, o].reshape(half, depth))
        return jnp.concatenate([high, high, low], axis=1)

    def multiply(pair, sources):
        for o in range(2):
            places = [(u, r, s, lax.rem(o + crossed[r], 2)) for u, (s, crossed) in enumerate(sources) for r in range(2)]
            lefts = jnp.concatenate([left(s, r, w) for _, r, s, w in places], axis=0)
            product = jnp.dot(lefts, weight[o], preferred_element_type=F32)
            for i, (u, r, _, w) in enumerate(places):
                total[pair, u, r, w] = product[i * half : (i + 1) * half]

    def crossings(s):
        return jnp.where(plane < s, 1, 0), jnp.where(plane + s < planes, 1, 0)

    def core_copy(pair, n):
        return pltpu.make_async_remote_copy(
            src_ref=total.at[pair, pl.ds(0, n), 1 - core], dst_ref=core_in.at[pair, pl.ds(0, n)],
            send_sem=core_send.at[pair], recv_sem=core_recv.at[pair], device_id=twin, device_id_type=MESH,
        )

    def plane_copy(pair, n, distance):
        there = lax.rem(group + distance % groups, groups)
        return pltpu.make_async_remote_copy(
            src_ref=core_sum.at[pair, pl.ds(0, n), distance // groups, pl.ds(pl.multiple_of(there * rows, rows), rows)],
            dst_ref=plane_in.at[pair, distance - 1, pl.ds(0, n)],
            send_sem=plane_send.at[pair], recv_sem=plane_recv.at[pair],
            device_id=plane_peer(distance), device_id_type=MESH,
        )

    def plane_all(pair, n):
        everything = plane_in.at[pair, :, pl.ds(0, n)]
        return pltpu.make_async_remote_copy(
            src_ref=everything, dst_ref=everything, send_sem=plane_send.at[pair], recv_sem=plane_recv.at[pair],
            device_id=across, device_id_type=MESH,
        )

    def home_copy(pair, u, s, which):
        out = (margin_ref, hamilton_ref)[which]
        k = s + core * (planes - 2 * s)
        return pltpu.make_async_remote_copy(
            src_ref=result.at[pair, u, :, pl.ds(which * width, width)],
            dst_ref=out.at[:, pl.ds(pl.multiple_of(k * width, width), width)],
            send_sem=home_send.at[k, which], recv_sem=home_recv.at[k, which],
            device_id=at_plane((2 * core - 1) * s), device_id_type=MESH,
        )

    def to_twin(pair, n):
        core_copy(pair, n).start()

    def sum_cores(pair, n):
        core_copy(pair, n).wait_recv()
        for u in range(n):
            for o in range(2):
                core_sum[pair, u, o] = total[pair, u, core, o] + core_in[pair, u, o]

    def to_plane(pair, n, distances):
        for d in distances:
            plane_copy(pair, n, d).start()

    peers = range(1, 2 * groups)

    def summed(pair, u):
        value = core_sum[pair, u, 0, pl.ds(pl.multiple_of(group * rows, rows), rows), :]
        for d in peers:
            value = value + plane_in[pair, d - 1, u]
        return value

    def sum_plane(pair, n):
        plane_all(pair, n).wait_recv()
        for u in range(n):
            result[pair, u] = summed(pair, u)

    def to_home(pair, n):
        for u in range(n):
            for which in range(2):
                home_copy(pair, u, 2 * pair - 1 + u, which).start()

    def stay_home():
        plane_all(0, 2).wait_recv()
        for u, k in ((0, 0), (1, planes)):
            value = summed(0, u)
            margin_ref[:, pl.ds(k * width, width)] = value[:, :width]
            hamilton_ref[:, pl.ds(k * width, width)] = value[:, width:]

    def multiply_pair(pair):
        multiply(pair, [(s, crossings(s)) for s in (2 * pair - 1, 2 * pair)])

    for j in range(parts):
        pass_on(1, 0, j)
        for r in range(2):
            hand_across(r, j).wait_recv()
            ring(0, r, 1, j).start()
    for s, o in ((1, 1), (2, 0), (2, 1)):
        for j in range(parts):
            pass_on(s, o, j)

    def two_steps(pair, _):
        def work(event):
            if event == 0:
                @pl.when(pair == 3)
                def _():
                    sum_cores(0, 2)
                    to_plane(0, 2, peers)
            if event == 3:
                @pl.when(pair == 2)
                def _():
                    for i in range(2):
                        hand_image(i).wait_recv()
                        weigh(1, image[i], slice(i * width, (i + 1) * width))
            if event == 4:
                multiply_pair(pair - 1)
                to_twin(pair - 1, 2)
            if event == 5:
                @pl.when(pair == 2)
                def _():
                    multiply(0, [(0, (0, 0)), (0, (1, 1))])
                    to_twin(0, 2)

                @pl.when(pair > 2)
                def _():
                    sum_plane(pair - 2, 2)
            if event == 6:
                sum_cores(pair - 1, 2)
                to_plane(pair - 1, 2, peers[: len(peers) // 2])
            if event == 7:
                to_plane(pair - 1, 2, peers[len(peers) // 2 :])

        events = 4 * parts
        for event in range(events):
            step, o, j = event // (2 * parts), event // parts % 2, event % parts
            pass_on(2 * pair - 1 + step, o, j)
            for e in range(event * 8 // events, (event + 1) * 8 // events):
                work(e)
        return 0

    lax.fori_loop(2, pairs, two_steps, 0)
    multiply_pair(pairs - 1)
    to_twin(pairs - 1, 2)

    def go_home(pair, _):
        to_home(pair, 2)
        return 0

    lax.fori_loop(1, pairs - 2, go_home, 0)
    sum_cores(pairs - 1, 2)
    to_plane(pairs - 1, 2, peers)
    for o in range(2):
        for j in range(parts):
            for r in range(2):
                ring(planes - 2, r, o, j).wait_recv()
    multiply(pairs, [(planes - 1, crossings(planes - 1))])
    to_twin(pairs, 1)
    sum_plane(pairs - 2, 2)
    to_home(pairs - 2, 2)
    sum_cores(pairs, 1)
    to_plane(pairs, 1, peers)

    def ring_sent(s, _):
        for r in range(2):
            for o in range(2):
                for j in range(parts):
                    ring(s, r, o, j).wait_send()
        return 0

    lax.fori_loop(0, planes - 1, ring_sent, 0)
    for r in range(2):
        hand_image(r).wait_send()
        for j in range(parts):
            hand_across(r, j).wait_send()

    def sums_sent(pair, _):
        core_copy(pair, 2).wait_send()
        plane_all(pair, 2).wait_send()
        return 0

    lax.fori_loop(0, pairs, sums_sent, 0)
    stay_home()
    sum_plane(pairs - 1, 2)
    to_home(pairs - 1, 2)
    sum_plane(pairs, 1)
    to_home(pairs, 1)
    core_copy(pairs, 1).wait_send()
    plane_all(pairs, 1).wait_send()

    def home_done(s, _):
        for which in range(2):
            home_copy(0, 0, s, which).wait()
        return 0

    lax.fori_loop(1, planes, home_done, 0)


def solution(mesh):
    bands, slabs = mesh.shape["band"], mesh.shape["pw"]
    planes, groups = bands // 2, slabs // 2
    pairs, parts = planes // 2, 2

    def shards(psi, h):
        depth, width = psi.shape[0] // 2, psi.shape[1]
        half, rows = width // 2, width // slabs
        out = jax.ShapeDtypeStruct((rows, (planes + 1) * width), F32)
        vmem, anywhere = pl.BlockSpec(memory_space=pltpu.VMEM), pl.BlockSpec(memory_space=pl.ANY)
        dma = pltpu.SemaphoreType.DMA
        return pl.pallas_call(
            functools.partial(kernel, bands, slabs),
            out_shape=(out, out),
            in_specs=[anywhere, anywhere],
            out_specs=(vmem, vmem),
            scratch_shapes=[
                pltpu.VMEM(psi.shape, F32),
                pltpu.VMEM(h.shape, F32),
                pltpu.VMEM((2, parts, half // parts, depth), F32),
                pltpu.VMEM((2, depth, width), F32),
                pltpu.VMEM((planes, 2, 2, parts, half // parts, depth), F32),
                pltpu.VMEM((2, 3 * depth, 2 * width), BF16),
                pltpu.VMEM((pairs + 1, 2, 2, 2, half, 2 * width), F32),
                pltpu.VMEM((pairs + 1, 2, 2, half, 2 * width), F32),
                pltpu.VMEM((pairs + 1, 2, 2, half, 2 * width), F32),
                pltpu.VMEM((pairs + 1, 2 * groups - 1, 2, rows, 2 * width), F32),
                pltpu.VMEM((pairs + 1, 2, rows, 2 * width), F32),
                dma((2,)),
                dma((planes - 1, 2, 2, parts)),
                dma((planes, 2, 2, parts)),
                dma((2, parts)),
                dma((2, parts)),
                dma((2,)),
                dma((2,)),
                dma((pairs + 1,)),
                dma((pairs + 1,)),
                dma((pairs + 1,)),
                dma((pairs + 1,)),
                dma((planes, 2)),
                dma((planes, 2)),
            ],
            compiler_params=pltpu.CompilerParams(
                collective_id=0, has_side_effects=True, vmem_limit_bytes=54900 << 10
            ),
            cost_estimate=pl.CostEstimate(
                flops=6 * (planes + 1) * 2 * depth * width * 2 * width,
                bytes_accessed=4 * (4 * depth * width + 2 * rows * (planes + 1) * width),
                transcendentals=0,
            ),
        )(psi, h)

    return jax.shard_map(
        shards,
        mesh=mesh,
        in_specs=(P("pw", "band"), P("pw", "band")),
        out_specs=(P(("band", "pw"), None), P(("band", "pw"), None)),
        check_vma=False,
    )
```

time: 105 us -> 97.8 us (0.931)
  Pallas kernels: 101 us -> 95.8 us
  local copies, waits for them, and re-layouts: 3.25 us -> 1.26 us
    pallas_call x1, Pallas kernels: 101 us -> 95.8 us  [shards(): pl.pallas_call(functools.partial(kernel, bands, slabs), out_shape=(out, o...]
    unnamed x6 -> x2, local copies, waits for them, and re-layouts: 3.25 us -> 1.26 us
where the time goes in v3:
time: 97.8 us; the launch traced here: 97.7 us
  Pallas kernels  95.8 us (98%)
  local copies, waits for them, and re-layouts  1.26 us (1%)
    pallas_call x1, Pallas kernels, shards(): pl.pallas_call(functools.partial(kernel, bands, slabs), out_shape=(out, o...  95.8 us

profile of v3, /device:TPU:1, one launch (start us, length us, event | category | flops | bytes accessed | tf_op | source)
XLA Modules:
  0.0 97.7 jit_solution(4663408981934726911)
XLA Ops:
  0.6 95.8 %shard_map.41 = (f32[8,2176]{1,0:T(8,128)S(1)}, f32[8,2176]{1,0:T(8,128)S(1)}) custom-call(f32[768,128]{1,0:T(8,128)} %psi_hbm.1, f32[768,128]{1,0:T(8,128)} %h_hbm.1), custom_call_target="tpu_custom_call" | custom-call | flops 2566914048 | bytes 925696 | tf_op jit(solution)/shard_map/pallas_call | solution.py:315
  96.4 0.6 copy.6
  97.1 0.6 copy.7

commit v4 on v3

--- a/solution.py
+++ b/solution.py
@@ -18,12 +18,13 @@
 
 def kernel(
     bands, slabs, psi_hbm, h_hbm, margin_ref, hamilton_ref,
-    psi, h, turned_away, image, block, weight, total, core_in, core_sum, plane_in, result,
+    psi, h, turned_away, image, block, weight, total, core_in, core_sum, plane_in, result, home_in, direct_in,
     load_sem, ring_send, ring_recv, across_send, across_recv, image_send, image_recv,
-    core_send, core_recv, plane_send, plane_recv, home_send, home_recv,
+    core_send, core_recv, plane_send, plane_recv, home_send, home_recv, direct_send, direct_recv,
 ):
     planes, groups = bands // 2, slabs // 2
-    pairs = planes // 2
+    pairs = planes // 2 - 1
+    end = planes - 1
     parts = block.shape[3]
     depth, width = psi.shape[0] // 2, psi.shape[1]
     half = width // 2
@@ -91,8 +92,6 @@
         for r in range(2):
             ring(0, r, 0, j).start()
             hand_across(r, j).start()
-    for i in range(2):
-        hand_image(i).start()
 
     def weigh(o, values, lanes):
         high, low = split(values)
@@ -107,6 +106,9 @@
         for r in range(2):
             ring(s - 1, r, o, j).wait_recv()
             ring(s, r, o, j).start()
+        if not (isinstance(s, int) and s == 1):
+            for r in range(2):
+                ring(s - 1, r, o, j).wait_send()
 
     def left(s, r, o):
         high, low = split(block[s, r, o].reshape(half, depth))
@@ -145,21 +147,50 @@
             device_id=across, device_id_type=MESH,
         )
 
-    def home_copy(pair, u, s, which):
-        out = (margin_ref, hamilton_ref)[which]
+    def first_step(group_index):
+        return group_index + (end - pairs - 2) if isinstance(group_index, int) and group_index >= pairs else 2 * group_index - 1
+
+    def home_copy(pair, u, s):
         k = s + core * (planes - 2 * s)
         return pltpu.make_async_remote_copy(
-            src_ref=result.at[pair, u, :, pl.ds(which * width, width)],
-            dst_ref=out.at[:, pl.ds(pl.multiple_of(k * width, width), width)],
-            send_sem=home_send.at[k, which], recv_sem=home_recv.at[k, which],
+            src_ref=result.at[pair, u], dst_ref=home_in.at[k], send_sem=home_send.at[0], recv_sem=home_recv.at[0],
             device_id=at_plane((2 * core - 1) * s), device_id_type=MESH,
+        )
+
+    def home_all():
+        everything = home_in.at[pl.ds(1 + core, end - 1)]
+        return pltpu.make_async_remote_copy(
+            src_ref=everything, dst_ref=everything, send_sem=home_send.at[0], recv_sem=home_recv.at[0],
+            device_id=up, device_id_type=MESH,
+        )
+
+    def direct_copy(distance):
+        there = lax.rem(group + distance % groups, groups)
+        side_there = lax.rem(side + distance // groups, 2)
+        plane_there = lax.rem(plane + (2 * core - 1) * end + planes, planes)
+        return pltpu.make_async_remote_copy(
+            src_ref=core_sum.at[pairs + 2, 0, distance // groups, pl.ds(pl.multiple_of(there * rows, rows), rows)],
+            dst_ref=direct_in.at[distance], send_sem=direct_send.at[0], recv_sem=direct_recv.at[0],
+            device_id=(side_there * planes + plane_there, 2 * there + core), device_id_type=MESH,
+        )
+
+    def direct_all():
+        return pltpu.make_async_remote_copy(
+            src_ref=direct_in, dst_ref=direct_in, send_sem=direct_send.at[0], recv_sem=direct_recv.at[0],
+            device_id=up, device_id_type=MESH,
+        )
+
+    def half_copy(o):
+        return pltpu.make_async_remote_copy(
+            src_ref=total.at[pairs + 2, 0, 1 - core, o], dst_ref=core_in.at[pairs + 2, 0, o],
+            send_sem=core_send.at[pairs + 2 + o], recv_sem=core_recv.at[pairs + 2 + o], device_id=twin, device_id_type=MESH,
         )
 
     def to_twin(pair, n):
         core_copy(pair, n).start()
 
     def sum_cores(pair, n):
-        core_copy(pair, n).wait_recv()
+        core_copy(pair, n).wait()
         for u in range(n):
             for o in range(2):
                 core_sum[pair, u, o] = total[pair, u, core, o] + core_in[pair, u, o]
@@ -177,35 +208,52 @@
         return value
 
     def sum_plane(pair, n):
-        plane_all(pair, n).wait_recv()
+        plane_all(pair, n).wait()
         for u in range(n):
             result[pair, u] = summed(pair, u)
 
     def to_home(pair, n):
         for u in range(n):
-            for which in range(2):
-                home_copy(pair, u, 2 * pair - 1 + u, which).start()
+            home_copy(pair, u, first_step(pair) + u).start()
+
+    def deliver(k, value):
+        margin_ref[:, pl.ds(k * width, width)] = value[:, :width]
+        hamilton_ref[:, pl.ds(k * width, width)] = value[:, width:]
 
     def stay_home():
-        plane_all(0, 2).wait_recv()
-        for u, k in ((0, 0), (1, planes)):
-            value = summed(0, u)
-            margin_ref[:, pl.ds(k * width, width)] = value[:, :width]
-            hamilton_ref[:, pl.ds(k * width, width)] = value[:, width:]
+        plane_all(0, 2).wait()
+        deliver(0, summed(0, 0))
+        deliver(planes, summed(0, 1))
 
     def multiply_pair(pair):
         multiply(pair, [(s, crossings(s)) for s in (2 * pair - 1, 2 * pair)])
+
+    def multiply_single(pair):
+        s = first_step(pair)
+        multiply(pair, [(s, crossings(s))])
 
     for j in range(parts):
         pass_on(1, 0, j)
         for r in range(2):
             hand_across(r, j).wait_recv()
             ring(0, r, 1, j).start()
+    for i in range(2):
+        hand_image(i).start()
     for s, o in ((1, 1), (2, 0), (2, 1)):
         for j in range(parts):
             pass_on(s, o, j)
 
-    def two_steps(pair, _):
+    front, back = peers[: len(peers) // 2], peers[len(peers) // 2 :]
+
+    def two_steps(pair, work):
+        events = 4 * parts
+        for event in range(events):
+            step, o, j = event // (2 * parts), event // parts % 2, event % parts
+            pass_on(2 * pair - 1 + step, o, j)
+            for e in range(event * 8 // events, (event + 1) * 8 // events):
+                work(e)
+
+    def turn_of(pair, _):
         def work(event):
             if event == 0:
                 @pl.when(pair == 3)
@@ -230,81 +278,111 @@
                 @pl.when(pair > 2)
                 def _():
                     sum_plane(pair - 2, 2)
+
+                @pl.when((pair > 2) & (pair < pairs - 2))
+                def _():
+                    to_home(pair - 2, 2)
+                @pl.when(pair == 4)
+                def _():
+                    stay_home()
             if event == 6:
                 sum_cores(pair - 1, 2)
-                to_plane(pair - 1, 2, peers[: len(peers) // 2])
+                to_plane(pair - 1, 2, front)
             if event == 7:
-                to_plane(pair - 1, 2, peers[len(peers) // 2 :])
-
-        events = 4 * parts
-        for event in range(events):
-            step, o, j = event // (2 * parts), event // parts % 2, event % parts
-            pass_on(2 * pair - 1 + step, o, j)
-            for e in range(event * 8 // events, (event + 1) * 8 // events):
-                work(e)
+                to_plane(pair - 1, 2, back)
+
+        two_steps(pair, work)
         return 0
 
-    lax.fori_loop(2, pairs, two_steps, 0)
-    multiply_pair(pairs - 1)
-    to_twin(pairs - 1, 2)
+    lax.fori_loop(2, pairs, turn_of, 0)
+
+    def last_turn(event):
+        if event == 0:
+            multiply_pair(pairs - 1)
+            to_twin(pairs - 1, 2)
+        if event == 1:
+            sum_plane(pairs - 2, 2)
+        if event == 2:
+            sum_cores(pairs - 1, 2)
+            to_plane(pairs - 1, 2, front)
+        if event == 3:
+            to_plane(pairs - 1, 2, back)
+        if event == 4:
+            multiply_single(pairs)
+            to_twin(pairs, 1)
+        if event == 6:
+            sum_cores(pairs, 1)
+            to_plane(pairs, 1, front)
+        if event == 7:
+            to_plane(pairs, 1, back)
+
+    two_steps(pairs, last_turn)
+    multiply_single(pairs + 1)
+    to_twin(pairs + 1, 1)
 
     def go_home(pair, _):
         to_home(pair, 2)
         return 0
 
-    lax.fori_loop(1, pairs - 2, go_home, 0)
-    sum_cores(pairs - 1, 2)
-    to_plane(pairs - 1, 2, peers)
+    lax.fori_loop(pairs - 4, pairs - 1, go_home, 0)
+    sum_cores(pairs + 1, 1)
+    to_plane(pairs + 1, 1, peers)
+
+    crossed = crossings(end)
     for o in range(2):
         for j in range(parts):
             for r in range(2):
-                ring(planes - 2, r, o, j).wait_recv()
-    multiply(pairs, [(planes - 1, crossings(planes - 1))])
-    to_twin(pairs, 1)
-    sum_plane(pairs - 2, 2)
-    to_home(pairs - 2, 2)
-    sum_cores(pairs, 1)
-    to_plane(pairs, 1, peers)
-
-    def ring_sent(s, _):
+                ring(end - 1, r, o, j).wait_recv()
         for r in range(2):
-            for o in range(2):
-                for j in range(parts):
-                    ring(s, r, o, j).wait_send()
-        return 0
-
-    lax.fori_loop(0, planes - 1, ring_sent, 0)
+            product = jnp.dot(left(end, r, o), weight[lax.rem(o + crossed[r], 2)], preferred_element_type=F32)
+            total[pairs + 2, 0, r, o] = product
+        half_copy(o).start()
+        if o == 0:
+            sum_plane(pairs - 1, 2)
+            to_home(pairs - 1, 2)
+            half_copy(o).wait_recv()
+            core_sum[pairs + 2, 0, o] = total[pairs + 2, 0, core, o] + core_in[pairs + 2, 0, o]
+            for d in range(groups):
+                direct_copy(d).start()
+    sum_plane(pairs, 1)
+    to_home(pairs, 1)
+    half_copy(1).wait_recv()
+    core_sum[pairs + 2, 0, 1] = total[pairs + 2, 0, core, 1] + core_in[pairs + 2, 0, 1]
+    for d in range(groups, 2 * groups):
+        direct_copy(d).start()
+    sum_plane(pairs + 1, 1)
+    to_home(pairs + 1, 1)
+
     for r in range(2):
         hand_image(r).wait_send()
         for j in range(parts):
             hand_across(r, j).wait_send()
-
-    def sums_sent(pair, _):
-        core_copy(pair, 2).wait_send()
-        plane_all(pair, 2).wait_send()
-        return 0
-
-    lax.fori_loop(0, pairs, sums_sent, 0)
-    stay_home()
-    sum_plane(pairs - 1, 2)
-    to_home(pairs - 1, 2)
-    sum_plane(pairs, 1)
-    to_home(pairs, 1)
-    core_copy(pairs, 1).wait_send()
-    plane_all(pairs, 1).wait_send()
-
-    def home_done(s, _):
-        for which in range(2):
-            home_copy(0, 0, s, which).wait()
-        return 0
-
-    lax.fori_loop(1, planes, home_done, 0)
+            for o in range(2):
+                ring(0, r, o, j).wait_send()
+                ring(end - 1, r, o, j).wait_send()
+    for o in range(2):
+        half_copy(o).wait_send()
+    home_all().wait()
+    for k in range(2, end):
+        deliver(k, home_in[k])
+    for c in range(2):
+        @pl.when(core == c)
+        def _():
+            deliver(1 + c * (end - 1), home_in[1 + c * (end - 1)])
+    direct_all().wait()
+    value = direct_in[0]
+    for d in range(1, 2 * groups):
+        value = value + direct_in[d]
+    for c in range(2):
+        @pl.when(core == c)
+        def _():
+            deliver(end - c * (end - 1), value)
 
 
 def solution(mesh):
     bands, slabs = mesh.shape["band"], mesh.shape["pw"]
     planes, groups = bands // 2, slabs // 2
-    pairs, parts = planes // 2, 2
+    pairs, parts = planes // 2 - 1, 2
 
     def shards(psi, h):
         depth, width = psi.shape[0] // 2, psi.shape[1]
@@ -324,11 +402,13 @@
                 pltpu.VMEM((2, depth, width), F32),
                 pltpu.VMEM((planes, 2, 2, parts, half // parts, depth), F32),
                 pltpu.VMEM((2, 3 * depth, 2 * width), BF16),
-                pltpu.VMEM((pairs + 1, 2, 2, 2, half, 2 * width), F32),
-                pltpu.VMEM((pairs + 1, 2, 2, half, 2 * width), F32),
-                pltpu.VMEM((pairs + 1, 2, 2, half, 2 * width), F32),
-                pltpu.VMEM((pairs + 1, 2 * groups - 1, 2, rows, 2 * width), F32),
-                pltpu.VMEM((pairs + 1, 2, rows, 2 * width), F32),
+                pltpu.VMEM((pairs + 3, 2, 2, 2, half, 2 * width), F32),
+                pltpu.VMEM((pairs + 3, 2, 2, half, 2 * width), F32),
+                pltpu.VMEM((pairs + 3, 2, 2, half, 2 * width), F32),
+                pltpu.VMEM((pairs + 3, 2 * groups - 1, 2, rows, 2 * width), F32),
+                pltpu.VMEM((pairs + 3, 2, rows, 2 * width), F32),
+                pltpu.VMEM((planes, rows, 2 * width), F32),
+                pltpu.VMEM((2 * groups, rows, 2 * width), F32),
                 dma((2,)),
                 dma((planes - 1, 2, 2, parts)),
                 dma((planes, 2, 2, parts)),
@@ -336,12 +416,14 @@
                 dma((2, parts)),
                 dma((2,)),
                 dma((2,)),
-                dma((pairs + 1,)),
-                dma((pairs + 1,)),
-                dma((pairs + 1,)),
-                dma((pairs + 1,)),
-                dma((planes, 2)),
-                dma((planes, 2)),
+                dma((pairs + 4,)),
+                dma((pairs + 4,)),
+                dma((pairs + 4,)),
+                dma((pairs + 4,)),
+                dma((1,)),
+                dma((1,)),
+                dma((1,)),
+                dma((1,)),
             ],
             compiler_params=pltpu.CompilerParams(
                 collective_id=0, has_side_effects=True, vmem_limit_bytes=54900 << 10

time: 97.8 us -> 97.2 us (level)
  no operation moved by 1% of the time
where the time goes in v4:
time: 97.2 us; the launch traced here: 96.8 us
  Pallas kernels  94.9 us (98%)
  local copies, waits for them, and re-layouts  1.26 us (1%)
    pallas_call x1, Pallas kernels, shards(): pl.pallas_call(functools.partial(kernel, bands, slabs), out_shape=(out, o...  94.9 us

profile of v4, /device:TPU:1, one launch (start us, length us, event | category | flops | bytes accessed | tf_op | source)
XLA Modules:
  0.0 96.8 jit_solution(11327132235087047533)
XLA Ops:
  0.6 94.9 %shard_map.41 = (f32[8,2176]{1,0:T(8,128)S(1)}, f32[8,2176]{1,0:T(8,128)S(1)}) custom-call(f32[768,128]{1,0:T(8,128)} %psi_hbm.1, f32[768,128]{1,0:T(8,128)} %h_hbm.1), custom_call_target="tpu_custom_call" | custom-call | flops 2566914048 | bytes 925696 | tf_op jit(solution)/shard_map/pallas_call | solution.py:393
  95.5 0.6 copy.6
  96.2 0.6 copy.7

commit v5 on v4

--- a/solution.py
+++ b/solution.py
@@ -199,7 +199,8 @@
         for d in distances:
             plane_copy(pair, n, d).start()
 
-    peers = range(1, 2 * groups)
+    around = sorted(range(groups), key=lambda d: -min(d, groups - d))
+    peers = sorted(range(1, 2 * groups), key=lambda d: -min(d % groups, -d % groups) - d // groups * (groups // 2))
 
     def summed(pair, u):
         value = core_sum[pair, u, 0, pl.ds(pl.multiple_of(group * rows, rows), rows), :]
@@ -342,14 +343,14 @@
             to_home(pairs - 1, 2)
             half_copy(o).wait_recv()
             core_sum[pairs + 2, 0, o] = total[pairs + 2, 0, core, o] + core_in[pairs + 2, 0, o]
-            for d in range(groups):
+            for d in around:
                 direct_copy(d).start()
     sum_plane(pairs, 1)
     to_home(pairs, 1)
     half_copy(1).wait_recv()
     core_sum[pairs + 2, 0, 1] = total[pairs + 2, 0, core, 1] + core_in[pairs + 2, 0, 1]
-    for d in range(groups, 2 * groups):
-        direct_copy(d).start()
+    for d in around:
+        direct_copy(groups + d).start()
     sum_plane(pairs + 1, 1)
     to_home(pairs + 1, 1)
 

time: 97.2 us -> 96.9 us (level)
  no operation moved by 1% of the time
where the time goes in v5:
time: 96.9 us; the launch traced here: 96.8 us
  Pallas kernels  94.9 us (98%)
  local copies, waits for them, and re-layouts  1.26 us (1%)
    pallas_call x1, Pallas kernels, shards(): pl.pallas_call(functools.partial(kernel, bands, slabs), out_shape=(out, o...  94.9 us

profile of v5, /device:TPU:1, one launch (start us, length us, event | category | flops | bytes accessed | tf_op | source)
XLA Modules:
  0.0 96.8 jit_solution(2156220152415968152)
XLA Ops:
  0.6 94.9 %shard_map.41 = (f32[8,2176]{1,0:T(8,128)S(1)}, f32[8,2176]{1,0:T(8,128)S(1)}) custom-call(f32[768,128]{1,0:T(8,128)} %psi_hbm.1, f32[768,128]{1,0:T(8,128)} %h_hbm.1), custom_call_target="tpu_custom_call" | custom-call | flops 2566914048 | bytes 925696 | tf_op jit(solution)/shard_map/pallas_call | solution.py:394
  95.5 0.6 copy.6
  96.1 0.6 copy.7

commit v6 on v5

--- a/solution.py
+++ b/solution.py
@@ -200,7 +200,10 @@
             plane_copy(pair, n, d).start()
 
     around = sorted(range(groups), key=lambda d: -min(d, groups - d))
-    peers = sorted(range(1, 2 * groups), key=lambda d: -min(d % groups, -d % groups) - d // groups * (groups // 2))
+    peers = sorted(
+        range(1, 2 * groups),
+        key=lambda d: -min(d % groups, -d % groups) - 2 * (1 if d % 2 else d // groups * 2),
+    )
 
     def summed(pair, u):
         value = core_sum[pair, u, 0, pl.ds(pl.multiple_of(group * rows, rows), rows), :]

time: 96.9 us -> 96.6 us (level)
  no operation moved by 1% of the time
where the time goes in v6:
time: 96.6 us; the launch traced here: 96.5 us
  Pallas kernels  94.6 us (98%)
  local copies, waits for them, and re-layouts  1.26 us (1%)
    pallas_call x1, Pallas kernels, shards(): pl.pallas_call(functools.partial(kernel, bands, slabs), out_shape=(out, o...  94.6 us

profile of v6, /device:TPU:1, one launch (start us, length us, event | category | flops | bytes accessed | tf_op | source)
XLA Modules:
  0.0 96.5 jit_solution(6609065424584066483)
XLA Ops:
  0.6 94.6 %shard_map.41 = (f32[8,2176]{1,0:T(8,128)S(1)}, f32[8,2176]{1,0:T(8,128)S(1)}) custom-call(f32[768,128]{1,0:T(8,128)} %psi_hbm.1, f32[768,128]{1,0:T(8,128)} %h_hbm.1), custom_call_target="tpu_custom_call" | custom-call | flops 2566914048 | bytes 925696 | tf_op jit(solution)/shard_map/pallas_call | solution.py:397
  95.2 0.6 copy.6
  95.9 0.6 copy.7
